TPU v7x, 512 devices: a whole 4x4x16 slice. The times are simulated.
512 devices in a mesh: dp: 16 (over z_lo, x), panel: 32 (over y, z_hi, core).
Axes of the slice: x: 4, y: 4, z: 16 (z_hi: 4, z_lo: 4; z = z_hi * 4 + z_lo), core: 2. Of those that a mesh axis runs over, the one named last changes fastest.
Arguments:
- features: bfloat16 [12288, 4096], P('dp', 'panel'), may hold values from -48 to 48
- sketch: float32 [32, 128, 256], P('panel', 'dp'), may hold values from -6 to 6
- counts: int32 [16], replicated, may hold values from 384 to 768, as said below
Outputs:
- covariance: float32 [4096, 16, 256], P('panel', 'dp')
- basis: float32 [32, 128, 256], P('panel', 'dp')
Inputs may be any that keep to these rules, and one draw needn't show every extreme that they name: `counts`: some dp index has all 768 rows live.
All inputs are finite; a program needn't handle non-finite values.
Results may differ from a plain program's by a relative error of at most 0.0003.
Values may be sent and summed in bfloat16 or wider, within the bound.
No kernel may reach another device: no remote copies, remote signals or barrier semaphores. Data moves between devices by JAX's collectives and lax.ppermute only.
A program may use at most 64 MiB of HBM per device.

v0:
```python
import math
import jax
import jax.numpy as jnp
from jax import lax
from jax.sharding import PartitionSpec as P

ITERS = 2


def local(features, sketch, counts):
    dp_count = lax.axis_size("dp")
    panel_count = lax.axis_size("panel")
    tok_rows, feat_width = features.shape
    sub_rows = sketch.shape[1]
    rank_cols = sketch.shape[2]
    total_width = feat_width * panel_count
    limit = counts[lax.axis_index("dp")]
    live_rows = (lax.iota(jnp.int32, tok_rows) < limit).astype(jnp.bfloat16)
    masked = features * live_rows[:, None]
    token_total = jnp.sum(counts).astype(jnp.float32)
    contract = (((0,), (0,)), ((), ()))
    partial_value = lax.dot_general(
        masked,
        lax.all_gather(features, "panel", axis=1, tiled=True),
        contract,
        preferred_element_type=jnp.float32,
    )
    partial_value = partial_value.reshape(feat_width, panel_count, dp_count, sub_rows)
    partial_value = jnp.transpose(partial_value, (0, 2, 1, 3)).reshape(
        feat_width, dp_count, panel_count * sub_rows
    )
    summed = lax.psum_scatter(partial_value, "dp", scatter_dimension=1, tiled=True)
    covariance = summed / token_total
    cov_flat = covariance.reshape(feat_width, panel_count * sub_rows)
    basis_now = sketch[0]
    for sweep in range(ITERS):
        shaped = jnp.dot(
            cov_flat,
            lax.all_gather(basis_now, "panel", axis=0, tiled=True),
            precision=lax.Precision.HIGHEST,
            preferred_element_type=jnp.float32,
        ).reshape(dp_count, sub_rows, rank_cols)
        basis_block = lax.psum_scatter(shaped, "dp", scatter_dimension=0, tiled=True)[0]
        inner_gram = jnp.dot(
            basis_block.T,
            basis_block,
            precision=lax.Precision.HIGHEST,
            preferred_element_type=jnp.float32,
        )
        summed_gram = lax.psum(inner_gram, ("dp", "panel"))
        factor_low = jnp.linalg.cholesky(summed_gram)
        basis_now = jax.scipy.linalg.solve_triangular(factor_low, basis_block.T, lower=True).T
    scaled = (math.sqrt(total_width) * basis_now)[None]
    return (covariance, scaled)


def solution(mesh):
    in_specs = (P("dp", "panel"), P("panel", "dp", None), P())
    out_specs = (P("panel", "dp", None), P("panel", "dp", None))
    return jax.shard_map(local, mesh=mesh, in_specs=in_specs, out_specs=out_specs, check_vma=False)
```

profile of v0, /device:TPU:4, one launch (start us, length us, event | category | flops | bytes accessed | tf_op | source)
XLA Modules:
  0.0 1509.2 jit_solution(8885281473320648278)
XLA Ops:
  9.9 128.8 %all-gather.3.cloned.1.call-done = bf16[768,4096]{1,0:T(8,128)(2,1)} async-done(((bf16[768,128]{1,0:T(8,128)(2,1)}), bf16[768,4096]{1,0:T(8,128)(2,1)}) %all-gather.3.cloned.1.call-update) | async-done | bytes 6291472 | tf_op jit(solution)/shard_map/all_gather | solution.py:24
  138.7 5.6 fusion.6
  144.4 1.6 copy.31
  147.3 49.7 %all-gather = f32[1,256,256]{2,1,0:T(8,128)S(1)} all-gather(f32[1,8,256]{2,1,0:T(8,128)S(1)} %copy-done), channel_id=2, replica_groups=mesh['dp'=16,'panel'=32] {'panel'}, dimensions={1}, use_global_device_ids=true | all-gather | bytes 270336 | tf_op jit(solution)/shard_map/all_gather | solution.py:39
  197.0 31.1 %reduce-scatter.4.cloned.1.call-done = f32[128,1,256]{0,2,1:T(8,128)} async-done(((f32[128,16,256]{0,2,1:T(8,128)}), f32[128,1,256]{0,2,1:T(8,128)}) %reduce-scatter.4.cloned.1.call-update) | async-done | bytes 131088 | tf_op jit(solution)/shard_map/reduce_scatter | solution.py:32
  230.2 86.6 %reduce-scatter.6.cloned.1.call-done = f32[1,8,256]{2,1,0:T(8,128)} async-done(((f32[16,8,256]{2,1,0:T(8,128)}), f32[1,8,256]{2,1,0:T(8,128)}) %reduce-scatter.6.cloned.1.call-update) | async-done | bytes 8208 | tf_op jit(solution)/shard_map/reduce_scatter | solution.py:43
  316.7 1.9 fusion.30
  318.9 462.3 %all-reduce.4.cloned.1.call-done = f32[256,256]{0,1:T(8,128)} async-done(((f32[256,256]{0,1:T(8,128)}), f32[256,256]{0,1:T(8,128)}) %all-reduce.4.cloned.1.call-update) | async-done | bytes 262160 | tf_op jit(solution)/shard_map/psum | solution.py:50
  783.3 11.7 cholesky.130
  795.1 9.8 custom-call.13
  805.4 11.7 cholesky.147
  819.2 4.1 while.4
  819.9 1.3 bitcast_dynamic-update-slice_fusion.4
  822.0 1.3 bitcast_dynamic-update-slice_fusion.4
  823.3 19.7 %custom-call.14 = f32[2,128,128]{1,2,0:T(8,128)S(1)} custom-call(f32[2,128,128]{2,1,0:T(8,128)S(1)} %get-tuple-element.18), custom_call_target="InvertDiagBlocksLowerTriangular" | custom-call | tf_op jit(solution)/shard_map/jit(_solve_triangular)/triangular_solve | solution.py:52
  844.9 51.6 %all_gather.11 = f32[256,256]{1,0:T(8,128)S(1)} all-gather(f32[8,256]{1,0:T(8,128)S(1)} %maximum_bitcast_fusion), channel_id=1, replica_groups=mesh['dp'=16,'panel'=32] {'panel'}, dimensions={0}, use_global_device_ids=true | all-gather | bytes 270336 | tf_op jit(solution)/shard_map/all_gather | solution.py:39
  897.7 75.2 %reduce-scatter.8.cloned.1.call-done = f32[1,8,256]{2,1,0:T(8,128)} async-done(((f32[16,8,256]{2,1,0:T(8,128)}), f32[1,8,256]{2,1,0:T(8,128)}) %reduce-scatter.8.cloned.1.call-update) | async-done | bytes 8208 | tf_op jit(solution)/shard_map/reduce_scatter | solution.py:43
  972.9 1.9 fusion.28
  975.6 461.6 %all-reduce.6.cloned.1.call-done = f32[256,256]{0,1:T(8,128)} async-done(((f32[256,256]{0,1:T(8,128)}), f32[256,256]{0,1:T(8,128)}) %all-reduce.6.cloned.1.call-update) | async-done | bytes 262160 | tf_op jit(solution)/shard_map/psum | solution.py:50
  1439.3 11.7 cholesky.164
  1451.1 9.8 custom-call.15
  1461.4 11.7 cholesky.181
  1475.8 4.3 while.5
  1480.2 19.7 %custom-call.16 = f32[2,128,128]{1,2,0:T(8,128)S(1)} custom-call(f32[2,128,128]{2,1,0:T(8,128)S(1)} %get-tuple-element.19), custom_call_target="InvertDiagBlocksLowerTriangular" | custom-call | tf_op jit(solution)/shard_map/jit(_solve_triangular)/triangular_solve | solution.py:52
  (67 shorter events, 24.9 us)
Async XLA Ops:
  7.2 131.6 %all-gather.3.cloned.1.call-start = ((), (), s32[]{:S(2)}) async-start(), calls=%async_computation.3 | async-start | bytes 6488064 | tf_op jit(solution)/shard_map/all_gather | solution.py:24
  7.9 220.2 %reduce-scatter.4.cloned.1.call-start = ((), (), s32[]{:S(2)}) async-start(), calls=%async_computation.4 | async-start | bytes 2228224 | tf_op jit(solution)/shard_map/reduce_scatter | solution.py:32
  9.8 136.2 %copy-start.1 = (s32[16]{0:T(128)S(1)}, s32[16]{0:T(128)}, u32[]{:S(2)}) copy-start(s32[16]{0:T(128)} %param.8) | copy-start | bytes 196
  9.9 137.4 %copy-start = (f32[1,8,256]{2,1,0:T(8,128)S(1)}, f32[1,8,256]{2,1,0:T(8,128)}, u32[]{:S(2)}) copy-start(f32[1,8,256]{2,1,0:T(8,128)} %param.7) | copy-start | bytes 24580
  146.0 170.8 %reduce-scatter.6.cloned.1.call-start = ((), (), s32[]{:S(2)}) async-start(), calls=%async_computation.5 | async-start | bytes 139264 | tf_op jit(solution)/shard_map/reduce_scatter | solution.py:43
  230.1 551.1 %all-reduce.4.cloned.1.call-start = ((), (), s32[]{:S(2)}) async-start(), calls=%async_computation.6 | async-start | bytes 524288 | tf_op jit(solution)/shard_map/psum | solution.py:50
  318.7 654.3 %reduce-scatter.8.cloned.1.call-start = ((), (), s32[]{:S(2)}) async-start(), calls=%async_computation.7 | async-start | bytes 139264 | tf_op jit(solution)/shard_map/reduce_scatter | solution.py:43
  897.5 539.8 %all-reduce.6.cloned.1.call-start = ((), (), s32[]{:S(2)}) async-start(), calls=%async_computation.8 | async-start | bytes 524288 | tf_op jit(solution)/shard_map/psum | solution.py:50
Sparse Core Ops, SparseCore 0:
  11.1 127.6 all-gather.2
  146.1 82.0 reduce-scatter.3
  231.5 85.1 reduce-scatter.5
  322.9 458.2 all-reduce.3
  897.6 75.3 reduce-scatter.7
  979.1 458.0 all-reduce.5
where the time goes:
time: 1510 us
  waiting for transfers between devices  1250 us (83%)
  other arithmetic  113 us (7%)
  blocking collectives  101 us (7%)
  between operations  17.5 us (1%)
  matrix products  16.1 us (1%)
    psum x2, waiting for transfers between devices, local(): summed_gram = lax.psum(inner_gram, ('dp', 'panel'))  924 us
    reduce_scatter x2, waiting for transfers between devices, local(): lax.psum_scatter(shaped, 'dp', scatter_dimension=0, tiled=True)[0]  162 us
    all_gather x1, waiting for transfers between devices, local(): lax.all_gather(features, 'panel', axis=1, tiled=True)  129 us
    all_gather x2, blocking collectives, local(): lax.all_gather(basis_now, 'panel', axis=0, tiled=True)  101 us
    another operation x13, other arithmetic, local(): factor_low = jnp.linalg.cholesky(summed_gram)  68.7 us
    another operation x5, other arithmetic, local(): jax.scipy.linalg.solve_triangular(factor_low, basis_block.T, lower=True)  39.4 us
    reduce_scatter x1, waiting for transfers between devices, local(): lax.psum_scatter(partial_value, 'dp', scatter_dimension=1, tiled=True)  31.1 us
  transfers between devices with their start and end apart: 6, of which 6 were waited for; matrix products, arithmetic and copies ran while one was open for 0% of the time, Pallas kernels for 0%

commit v1 on v0

--- a/solution.py
+++ b/solution.py
@@ -47,7 +47,7 @@
             precision=lax.Precision.HIGHEST,
             preferred_element_type=jnp.float32,
         )
-        summed_gram = lax.psum(inner_gram, ("dp", "panel"))
+        summed_gram = lax.psum(lax.psum(inner_gram, "panel"), "dp")
         factor_low = jnp.linalg.cholesky(summed_gram)
         basis_now = jax.scipy.linalg.solve_triangular(factor_low, basis_block.T, lower=True).T
     scaled = (math.sqrt(total_width) * basis_now)[None]

time: 1510 us -> 1610 us (1.066)
  the two profiles are of different devices: /device:TPU:4 before, /device:TPU:8 now
where the time goes in v1:
time: 1610 us
  waiting for transfers between devices  1350 us (84%)
  other arithmetic  113 us (7%)
  blocking collectives  96.7 us (6%)
  between operations  17.5 us (1%)
  matrix products  16.1 us (1%)
    psum x4, waiting for transfers between devices, local(): summed_gram = lax.psum(lax.psum(inner_gram, 'panel'), 'dp')  1020 us
    reduce_scatter x2, waiting for transfers between devices, local(): lax.psum_scatter(shaped, 'dp', scatter_dimension=0, tiled=True)[0]  171 us
    all_gather x1, waiting for transfers between devices, local(): lax.all_gather(features, 'panel', axis=1, tiled=True)  129 us
    all_gather x2, blocking collectives, local(): lax.all_gather(basis_now, 'panel', axis=0, tiled=True)  96.7 us
    another operation x13, other arithmetic, local(): factor_low = jnp.linalg.cholesky(summed_gram)  68.7 us
    another operation x5, other arithmetic, local(): jax.scipy.linalg.solve_triangular(factor_low, basis_block.T, lower=True)  39.4 us
    reduce_scatter x1, waiting for transfers between devices, local(): lax.psum_scatter(partial_value, 'dp', scatter_dimension=1, tiled=True)  39 us
  transfers between devices with their start and end apart: 8, of which 8 were waited for; matrix products, arithmetic and copies ran while one was open for 0% of the time, Pallas kernels for 0%

profile of v1, /device:TPU:8, one launch (start us, length us, event | category | flops | bytes accessed | tf_op | source)
XLA Modules:
  0.0 1612.7 jit_solution(17695246071949664032)
XLA Ops:
  9.9 128.8 %all-gather.3.cloned.1.call-done = bf16[768,4096]{1,0:T(8,128)(2,1)} async-done(((bf16[768,128]{1,0:T(8,128)(2,1)}), bf16[768,4096]{1,0:T(8,128)(2,1)}) %all-gather.3.cloned.1.call-update) | async-done | bytes 6291472 | tf_op jit(solution)/shard_map/all_gather | solution.py:24
  138.7 5.6 fusion.6
  144.3 1.6 copy.31
  147.3 46.7 %all-gather = f32[1,256,256]{2,1,0:T(8,128)S(1)} all-gather(f32[1,8,256]{2,1,0:T(8,128)S(1)} %copy-done), channel_id=2, replica_groups=mesh['dp'=16,'panel'=32] {'panel'}, dimensions={1}, use_global_device_ids=true | all-gather | bytes 270336 | tf_op jit(solution)/shard_map/all_gather | solution.py:39
  194.0 39.0 %reduce-scatter.4.cloned.1.call-done = f32[128,1,256]{0,2,1:T(8,128)} async-done(((f32[128,16,256]{0,2,1:T(8,128)}), f32[128,1,256]{0,2,1:T(8,128)}) %reduce-scatter.4.cloned.1.call-update) | async-done | bytes 131088 | tf_op jit(solution)/shard_map/reduce_scatter | solution.py:32
  235.0 86.3 %reduce-scatter.6.cloned.1.call-done = f32[1,8,256]{2,1,0:T(8,128)} async-done(((f32[16,8,256]{2,1,0:T(8,128)}), f32[1,8,256]{2,1,0:T(8,128)}) %reduce-scatter.6.cloned.1.call-update) | async-done | bytes 8208 | tf_op jit(solution)/shard_map/reduce_scatter | solution.py:43
  321.3 1.9 fusion.30
  323.3 326.7 %all-reduce.6.cloned.1.call-done = f32[256,256]{0,1:T(8,128)} async-done(((f32[256,256]{0,1:T(8,128)}), f32[256,256]{0,1:T(8,128)}) %all-reduce.6.cloned.1.call-update) | async-done | bytes 262160 | tf_op jit(solution)/shard_map/psum | solution.py:50
  650.3 181.0 %all-reduce.8.cloned.1.call-done = f32[256,256]{0,1:T(8,128)} async-done(((f32[256,256]{0,1:T(8,128)}), f32[256,256]{0,1:T(8,128)}) %all-reduce.8.cloned.1.call-update) | async-done | bytes 262160 | tf_op jit(solution)/shard_map/psum | solution.py:50
  833.4 11.7 cholesky.130
  845.1 9.8 custom-call.13
  855.4 11.7 cholesky.147
  869.3 4.3 while.4
  873.6 19.7 %custom-call.14 = f32[2,128,128]{1,2,0:T(8,128)S(1)} custom-call(f32[2,128,128]{2,1,0:T(8,128)S(1)} %get-tuple-element.18), custom_call_target="InvertDiagBlocksLowerTriangular" | custom-call | tf_op jit(solution)/shard_map/jit(_solve_triangular)/triangular_solve | solution.py:52
  895.2 50.0 %all_gather.11 = f32[256,256]{1,0:T(8,128)S(1)} all-gather(f32[8,256]{1,0:T(8,128)S(1)} %maximum_bitcast_fusion), channel_id=1, replica_groups=mesh['dp'=16,'panel'=32] {'panel'}, dimensions={0}, use_global_device_ids=true | all-gather | bytes 270336 | tf_op jit(solution)/shard_map/all_gather | solution.py:39
  946.2 84.5 %reduce-scatter.8.cloned.1.call-done = f32[1,8,256]{2,1,0:T(8,128)} async-done(((f32[16,8,256]{2,1,0:T(8,128)}), f32[1,8,256]{2,1,0:T(8,128)}) %reduce-scatter.8.cloned.1.call-update) | async-done | bytes 8208 | tf_op jit(solution)/shard_map/reduce_scatter | solution.py:43
  1030.6 1.9 fusion.28
  1032.6 326.5 %all-reduce.10.cloned.1.call-done = f32[256,256]{0,1:T(8,128)} async-done(((f32[256,256]{0,1:T(8,128)}), f32[256,256]{0,1:T(8,128)}) %all-reduce.10.cloned.1.call-update) | async-done | bytes 262160 | tf_op jit(solution)/shard_map/psum | solution.py:50
  1359.9 180.8 %all-reduce.12.cloned.1.call-done = f32[256,256]{0,1:T(8,128)} async-done(((f32[256,256]{0,1:T(8,128)}), f32[256,256]{0,1:T(8,128)}) %all-reduce.12.cloned.1.call-update) | async-done | bytes 262160 | tf_op jit(solution)/shard_map/psum | solution.py:50
  1542.8 11.7 cholesky.164
  1554.6 9.8 custom-call.15
  1564.9 11.7 cholesky.181
  1579.3 4.3 while.5
  1583.6 19.7 %custom-call.16 = f32[2,128,128]{1,2,0:T(8,128)S(1)} custom-call(f32[2,128,128]{2,1,0:T(8,128)S(1)} %get-tuple-element.19), custom_call_target="InvertDiagBlocksLowerTriangular" | custom-call | tf_op jit(solution)/shard_map/jit(_solve_triangular)/triangular_solve | solution.py:52
  (73 shorter events, 27.4 us)
Async XLA Ops:
  7.2 131.5 %all-gather.3.cloned.1.call-start = ((), (), s32[]{:S(2)}) async-start(), calls=%async_computation.3 | async-start | bytes 6488064 | tf_op jit(solution)/shard_map/all_gather | solution.py:24
  7.9 225.1 %reduce-scatter.4.cloned.1.call-start = ((), (), s32[]{:S(2)}) async-start(), calls=%async_computation.4 | async-start | bytes 2228224 | tf_op jit(solution)/shard_map/reduce_scatter | solution.py:32
  9.8 136.1 %copy-start.1 = (s32[16]{0:T(128)S(1)}, s32[16]{0:T(128)}, u32[]{:S(2)}) copy-start(s32[16]{0:T(128)} %param.8) | copy-start | bytes 196
  9.9 137.4 %copy-start = (f32[1,8,256]{2,1,0:T(8,128)S(1)}, f32[1,8,256]{2,1,0:T(8,128)}, u32[]{:S(2)}) copy-start(f32[1,8,256]{2,1,0:T(8,128)} %param.7) | copy-start | bytes 24580
  145.9 175.4 %reduce-scatter.6.cloned.1.call-start = ((), (), s32[]{:S(2)}) async-start(), calls=%async_computation.5 | async-start | bytes 139264 | tf_op jit(solution)/shard_map/reduce_scatter | solution.py:43
  235.0 415.1 %all-reduce.6.cloned.1.call-start = ((), (), s32[]{:S(2)}) async-start(), calls=%async_computation.6 | async-start | bytes 524288 | tf_op jit(solution)/shard_map/psum | solution.py:50
  323.2 508.0 %all-reduce.8.cloned.1.call-start = ((), (), s32[]{:S(2)}) async-start(), calls=%async_computation.7 | async-start | bytes 524288 | tf_op jit(solution)/shard_map/psum | solution.py:50
  650.1 380.6 %reduce-scatter.8.cloned.1.call-start = ((), (), s32[]{:S(2)}) async-start(), calls=%async_computation.8 | async-start | bytes 139264 | tf_op jit(solution)/shard_map/reduce_scatter | solution.py:43
  946.1 413.0 %all-reduce.10.cloned.1.call-start = ((), (), s32[]{:S(2)}) async-start(), calls=%async_computation.9 | async-start | bytes 524288 | tf_op jit(solution)/shard_map/psum | solution.py:50
  1032.5 508.2 %all-reduce.12.cloned.1.call-start = ((), (), s32[]{:S(2)}) async-start(), calls=%async_computation.10 | async-start | bytes 524288 | tf_op jit(solution)/shard_map/psum | solution.py:50
Sparse Core Ops, SparseCore 0:
  11.1 127.5 all-gather.2
  146.0 86.9 reduce-scatter.3
  236.4 84.9 reduce-scatter.5
  324.3 325.6 all-reduce.5
  652.8 178.4 all-reduce.7
  946.2 84.3 reduce-scatter.7
  1033.5 325.5 all-reduce.9
  1362.3 178.4 all-reduce.11
